TPU v7x, 1024 devices: a whole 4x4x32 slice. The times are simulated.
1024 devices in a mesh: ctx: 64 (over x_hi, z), head: 16 (over y, x_lo, core).
Axes of the slice: x: 4 (x_hi: 2, x_lo: 2; x = x_hi * 2 + x_lo), y: 4, z: 32, core: 2. Of those that a mesh axis runs over, the one named last changes fastest.
Arguments:
- query_rows: bfloat16 [12288, 4096], P('ctx', 'head'), may hold values from -4.5 to 4.5
- key_rows: bfloat16 [12288, 512], P('ctx'), may hold values from -4.5 to 4.5
- value_rows: bfloat16 [12288, 512], P('ctx'), may hold values from -6 to 6
- w_out: bfloat16 [4096, 2048], P('head'), may hold values from -0.09375 to 0.09375
Outputs:
- mixed: bfloat16 [12288, 2048], P('ctx', 'head')
All inputs are finite; a program needn't handle non-finite values.
Results may differ from a plain program's by a relative error of at most 0.019.
Values may be sent and summed in bfloat16 or wider, within the bound.
A program may use at most 32 MiB of HBM per device.

v0:
```python
import math

import jax
import jax.numpy as jnp
from jax import lax
from jax.sharding import PartitionSpec as P

KVH = 4
HD = 128


negative = -1e30


def attend(state, queries_half, position_half, block_keys, block_values, key_start, score_scale):
    maximum, denominator, numerator = state
    key_count = block_keys.shape[0]
    scores = (
        jnp.einsum("thd,kd->thk", queries_half, block_keys, preferred_element_type=jnp.float32)
        * score_scale
    )
    key_positions = key_start + jnp.arange(key_count, dtype=jnp.int32)
    allowed = key_positions[None, None, :] <= position_half[:, None, None]
    scores = jnp.where(allowed, scores, negative)
    updated = jnp.maximum(maximum, jnp.max(scores, axis=2))
    weights = jnp.where(allowed, jnp.exp(scores - updated[:, :, None]), 0.0)
    factor = jnp.exp(maximum - updated)
    denominator = denominator * factor + jnp.sum(weights, axis=2)
    numerator = numerator * factor[:, :, None] + jnp.einsum(
        "thk,kd->thd",
        weights.astype(jnp.bfloat16),
        block_values,
        preferred_element_type=jnp.float32,
    )
    return (updated, denominator, numerator)


def on_device(query_rows, key_rows, value_rows, w_out):
    local_tokens = query_rows.shape[0]
    head_count = lax.axis_size("head")
    local_heads = query_rows.shape[1] // HD
    kv_head = lax.axis_index("head") * KVH // head_count
    own_keys = lax.dynamic_slice_in_dim(key_rows, kv_head * HD, HD, 1)
    own_values = lax.dynamic_slice_in_dim(value_rows, kv_head * HD, HD, 1)
    row_numbers = jnp.arange(local_tokens, dtype=jnp.int32)
    positions = lax.axis_index("ctx") * local_tokens + row_numbers
    heads_view = query_rows.reshape(local_tokens, local_heads, HD)
    half_rows = local_tokens // 2
    halves = [
        (heads_view[:half_rows], positions[:half_rows]),
        (heads_view[half_rows:], positions[half_rows:]),
    ]
    score_scale = 1.0 / math.sqrt(HD)
    initial = (
        jnp.full((half_rows, local_heads), negative, jnp.float32),
        jnp.zeros((half_rows, local_heads), jnp.float32),
        jnp.zeros((half_rows, local_heads, HD), jnp.float32),
    )
    piece_keys = lax.all_gather(own_keys, "ctx", axis=0, tiled=True)
    piece_values = lax.all_gather(own_values, "ctx", axis=0, tiled=True)
    piece_rows = piece_keys.shape[0]
    block_rows = math.gcd(piece_rows, local_tokens * max(1, 1024 // local_tokens))
    block_total = piece_rows // block_rows

    def one_block(block_number, states):
        block_start = block_number * block_rows
        block_keys = lax.dynamic_slice_in_dim(piece_keys, block_start, block_rows, 0)
        block_values = lax.dynamic_slice_in_dim(piece_values, block_start, block_rows, 0)
        results = []
        for (queries_half, position_half), state in zip(halves, states):
            state = attend(
                state,
                queries_half,
                position_half,
                block_keys,
                block_values,
                block_start,
                score_scale,
            )
            results.append(state)
        return tuple(results)

    states = lax.fori_loop(0, block_total, one_block, (initial, initial))
    pieces = [state[2] / state[1][:, :, None] for state in states]
    attended = (
        jnp.concatenate(pieces, axis=0).astype(jnp.bfloat16).reshape(local_tokens, local_heads * HD)
    )
    partial_sums = jnp.dot(attended, w_out, preferred_element_type=jnp.float32)
    return lax.psum_scatter(
        partial_sums.astype(jnp.bfloat16), "head", scatter_dimension=1, tiled=True
    )


def solution(mesh):
    placed = (P("ctx", "head"), P("ctx", None), P("ctx", None), P("head", None))
    return jax.shard_map(
        on_device, mesh=mesh, in_specs=placed, out_specs=P("ctx", "head"), check_vma=False
    )
```

profile of v0, /device:TPU:1, one launch (start us, length us, event | category | flops | bytes accessed | tf_op | source)
XLA Modules:
  0.0 950.9 jit_solution(2872390194234370601)
XLA Ops:
  6.5 1.5 constant_dynamic-slice_fusion.1
  8.1 1.4 constant_dynamic-slice_fusion
  10.6 274.8 %all-gather.3.cloned.1.call-done = bf16[12288,128]{1,0:T(8,128)(2,1)} async-done(((bf16[192,128]{1,0:T(8,128)(2,1)}), bf16[12288,128]{1,0:T(8,128)(2,1)}) %all-gather.3.cloned.1.call-update) | async-done | bytes 3145744 | tf_op jit(solution)/shard_map/all_gather | solution.py:59
  285.4 279.2 %all-gather.5.cloned.1.call-done = bf16[12288,128]{1,0:T(8,128)(2,1)} async-done(((bf16[192,128]{1,0:T(8,128)(2,1)}), bf16[12288,128]{1,0:T(8,128)(2,1)}) %all-gather.5.cloned.1.call-update) | async-done | bytes 3145744 | tf_op jit(solution)/shard_map/all_gather | solution.py:60
  564.6 289.9 %while.24 = (s32[]{:T(128)}, f32[96,2]{0,1:T(2,128)S(1)}, f32[96,2]{0,1:T(2,128)S(1)}, f32[96,2,128]{2,0,1:T(8,128)S(1)}, f32[96,2]{0,1:T(2,128)S(1)}, /*index=5...) while((s32[]{:T(128)}, f32[96,2]{0,1:T(2,128)S(1)}, ...), condition=%wide.region_5.6_spmd.clone, body=%wide.region_0.5_spmd.clone.sunk | while | flops 38598728 | bytes 1747445 | solution.py:83
  577.1 1.0 convolution_add_fusion.4
  586.2 1.0 convolution_add_fusion.4
  595.2 1.0 convolution_add_fusion.4
  604.3 1.0 convolution_add_fusion.4
  613.4 1.0 convolution_add_fusion.4
  622.4 1.0 convolution_add_fusion.4
  631.5 1.0 convolution_add_fusion.4
  640.5 1.0 convolution_add_fusion.4
  649.6 1.0 convolution_add_fusion.4
  658.7 1.0 convolution_add_fusion.4
  667.7 1.0 convolution_add_fusion.4
  676.8 1.0 convolution_add_fusion.4
  685.8 1.0 convolution_add_fusion.4
  694.9 1.0 convolution_add_fusion.4
  704.0 1.0 convolution_add_fusion.4
  713.0 1.0 convolution_add_fusion.4
  722.1 1.0 convolution_add_fusion.4
  731.2 1.0 convolution_add_fusion.4
  740.2 1.0 convolution_add_fusion.4
  749.3 1.0 convolution_add_fusion.4
  758.3 1.0 convolution_add_fusion.4
  767.4 1.0 convolution_add_fusion.4
  776.5 1.0 convolution_add_fusion.4
  785.5 1.0 convolution_add_fusion.4
  855.2 1.3 copy.21
  856.5 86.3 %reduce-scatter.4.cloned.1.call-done = bf16[128,192]{1,0:T(8,128)(2,1)} async-done(((bf16[2048,192]{1,0:T(8,128)(2,1)}), bf16[128,192]{1,0:T(8,128)(2,1)}) %reduce-scatter.4.cloned.1.call-update) | async-done | bytes 49168
  942.8 1.6 copy.22
  (829 shorter events, 260.4 us)
Async XLA Ops:
  6.5 848.2 %copy-start = (bf16[256,2048]{1,0:T(8,128)(2,1)S(1)}, bf16[256,2048]{1,0:T(8,128)(2,1)}, u32[]{:S(2)}) copy-start(bf16[256,2048]{1,0:T(8,128)(2,1)} %param.9) | copy-start | bytes 3145732
  6.5 278.9 %all-gather.3.cloned.1.call-start = ((), (), s32[]{:S(2)}) async-start(), calls=%async_computation.1 | async-start | bytes 3194880 | tf_op jit(solution)/shard_map/all_gather | solution.py:59
  8.1 556.5 %all-gather.5.cloned.1.call-start = ((), (), s32[]{:S(2)}) async-start(), calls=%async_computation.2 | async-start | bytes 3194880 | tf_op jit(solution)/shard_map/all_gather | solution.py:60
  9.6 933.2 %reduce-scatter.4.cloned.1.call-start = ((), (), s32[]{:S(2)}) async-start(), calls=%async_computation.3 | async-start | bytes 1114112
Sparse Core Ops, SparseCore 0:
  11.6 273.7 all-gather.2
  289.7 274.8 all-gather.4
  856.6 86.1 reduce-scatter.3
where the time goes:
time: 965 us; the launch traced here: 951 us
  waiting for transfers between devices  640 us (66%)
  matrix products  267 us (28%)
  other arithmetic  17.1 us (2%)
  between operations  13.2 us (1%)
    all_gather x1, waiting for transfers between devices, on_device(): piece_values = lax.all_gather(own_values, 'ctx', axis=0, tiled=True)  279 us
    all_gather x1, waiting for transfers between devices, on_device(): piece_keys = lax.all_gather(own_keys, 'ctx', axis=0, tiled=True)  275 us
    dot_general x128, matrix products, attend(): jnp.einsum('thk,kd->thd', weights.astype(jnp.bfloat16), block_values, pre...  134 us
    dot_general x128, matrix products, attend(): jnp.einsum('thd,kd->thk', queries_half, block_keys, preferred_element_typ...  133 us
    unnamed x4, waiting for transfers between devices  86.4 us
  transfers between devices with their start and end apart: 3, of which 3 were waited for; matrix products, arithmetic and copies ran while one was open for 0% of the time, Pallas kernels for 0%

commit v1 on v0

v1 whole, which is shorter than its diff:
```python
import math

import jax
import jax.numpy as jnp
from jax import lax
from jax.experimental import pallas as pl
from jax.experimental.pallas import tpu as pltpu
from jax.sharding import PartitionSpec as P

MESH = pl.DeviceIdType.MESH
HD = 128
RING = 32
TOK = 192
ROWS = 96
PIECE = 48
COLS = 4 * ROWS
FLOOR = -1e20
MASKED = -1e30
EXP2 = math.log2(math.e) / math.sqrt(HD)

OFFSET = {0: 0, 1: 1, 3: -1, 2: 2}
WAVES = [
    [(0, 0), (1, 0), (3, 0), (2, 0), (2, 7)],
    [(0, 1), (0, 7), (1, 1), (1, 7), (3, 1), (3, 7), (2, 1), (2, 6)],
    [(0, 2), (0, 6), (1, 2), (1, 6), (3, 2), (3, 6), (2, 2), (2, 5)],
    [(0, 3), (0, 5), (1, 3), (1, 5), (3, 3), (3, 5), (2, 3), (2, 4)],
    [(0, 4), (1, 4), (3, 4)],
]
ORDER = [chunk for wave in WAVES for chunk in wave]
PLACE = {chunk: place for place, chunk in enumerate(ORDER)}
SHIFT = [(OFFSET[g] + 4 * j) % RING for g, j in ORDER]
CHAIN = {0: [(4, (0, 7)), (-4, (0, 1))], 7: [(4, (0, 6))], 6: [(4, (0, 5))], 1: [(-4, (0, 2))], 2: [(-4, (0, 3))]}


def near(slot):
    steps = [(1, (3, slot)), (-1, (1, slot))]
    if slot in (0, 7, 6, 5):
        steps.append((2, (2, (slot - 1) % 8)))
    if slot in (0, 1, 2, 3):
        steps.append((-2, (2, slot)))
    return steps


def kernel(
    q_in, k_in, v_in, w_in, out,
    kv, q, w, acc, stats, sent, got, got_stats, parts, landed,
    load_sem, z_send, z_recv, last_send, pair_send, pair_recv, q_send, q_recv, w_send, w_recv,
    merge_send, merge_recv, sum_send, sum_recv,
):
    ctx, head = lax.axis_index("ctx"), lax.axis_index("head")
    x_hi, z = lax.div(ctx, RING), lax.rem(ctx, RING)
    y, x_lo, core = lax.div(head, 4), lax.rem(lax.div(head, 2), 2), lax.rem(head, 2)
    other = 1 - core
    pair = lax.div(head, 2)

    def along_z(step):
        return (x_hi * RING + lax.rem(z + step + RING, RING), head)

    def along_x(xi, kd):
        hi = 1 - x_hi if xi & 2 else x_hi
        lo = 1 - x_lo if xi & 1 else x_lo
        return (hi * RING + z, y * 4 + lo * 2 + kd)

    def in_slice(i2, kd):
        lo = 1 - x_lo if i2 & 1 else x_lo
        yy = y
        if i2 & 2:
            yy = yy + 1 - 2 * lax.rem(y, 2)
        if i2 & 4:
            yy = lax.rem(yy + 2, 4)
        return (ctx, yy * 4 + lo * 2 + kd)

    def remote(src, dst, send, recv, device):
        return pltpu.make_async_remote_copy(
            src_ref=src, dst_ref=dst, send_sem=send, recv_sem=recv, device_id=device, device_id_type=MESH
        )

    first = pl.multiple_of(x_lo * ROWS + core * PIECE, 16)
    column = pl.multiple_of(y * HD, HD)
    own_k = pltpu.make_async_copy(
        k_in.at[pl.ds(first, PIECE), pl.ds(column, HD)], kv.at[core, 0, :, pl.ds(0, HD)], load_sem.at[0]
    )
    own_v = pltpu.make_async_copy(
        v_in.at[pl.ds(first, PIECE), pl.ds(column, HD)], kv.at[core, 0, :, pl.ds(HD, HD)], load_sem.at[1]
    )
    own_q = pltpu.make_async_copy(
        q_in.at[pl.ds(pl.multiple_of(core * ROWS, 16), ROWS)], q.at[0, core], load_sem.at[2]
    )
    own_w = pltpu.make_async_copy(w_in, w.at[core], load_sem.at[3])
    own_k.start()
    own_v.start()
    own_q.start()
    own_w.start()

    barrier = pltpu.get_barrier_semaphore()
    peers = [along_z(step) for step in (4, -4, 2, -2, 1, -1)]
    peers += [along_x(xi, kd) for xi in (2, 3) for kd in (core, other)]
    peers += [in_slice(i2, kd) for i2 in range(8) for kd in (core, other) if (i2, kd is core) != (0, True)]
    for peer in peers:
        pl.semaphore_signal(barrier, inc=1, device_id=peer, device_id_type=MESH)
    acc[...] = jnp.zeros_like(acc)
    row = lax.broadcasted_iota(jnp.int32, stats.shape, 1)
    stats[...] = jnp.where(row == 0, FLOOR, 0.0).astype(jnp.float32)
    own_k.wait()
    own_v.wait()
    pl.semaphore_wait(barrier, len(peers))

    waiting = []

    def z_copy(slot, step, chunk):
        place = PLACE[chunk]
        return remote(
            kv.at[core, PLACE[(0, slot)]], kv.at[core, place], z_send.at[place], z_recv.at[place], along_z(step)
        )

    def pass_on(slot):
        for step, chunk in CHAIN.get(slot, []) + near(slot):
            copy = z_copy(slot, step, chunk)
            copy.start()
            waiting.append(copy)

    def arrived(chunk):
        place = PLACE[chunk]
        remote(
            kv.at[core, place], kv.at[core, place], z_send.at[place], z_recv.at[place], along_z(4)
        ).wait_recv()

    pass_on(0)

    q_copies = []
    for xi in (2, 3, 1, 0):
        for same in (True, False):
            if (xi, same) == (0, True):
                continue
            kd = core if same else other
            copy = remote(
                q_in.at[pl.ds(pl.multiple_of(kd * ROWS, 16), ROWS)],
                q.at[xi, core],
                q_send.at[xi, int(same)],
                q_recv.at[xi, int(same)],
                along_x(xi, kd),
            )
            copy.start()
            q_copies.append((xi, same, copy))
            waiting.append(copy)
    w_copy = remote(w_in, w.at[core], w_send, w_recv, in_slice(0, other))
    w_copy.start()
    waiting.append(w_copy)

    def exchange(wave):
        begin, count = PLACE[WAVES[wave][0]], len(WAVES[wave])
        piece = kv.at[core, pl.ds(begin, count)]
        copy = remote(piece, piece, pair_send.at[wave], pair_recv.at[wave], in_slice(0, other))
        copy.start()
        waiting.append(copy)
        theirs = kv.at[other, pl.ds(begin, count)]
        remote(theirs, theirs, pair_send.at[wave], pair_recv.at[wave], in_slice(0, other)).wait_recv()

    def attend(wave, xi, masked):
        begin, count = PLACE[WAVES[wave][0]], len(WAVES[wave])
        queries = jnp.concatenate(
            [q[xi, ks, :, e * HD : (e + 1) * HD] for ks in range(2) for e in range(2)], axis=0
        )
        scores, values = [], []
        for half in range(2):
            block = kv[half, begin : begin + count].reshape(count * PIECE, 2 * HD)
            s = lax.dot_general(
                block[:, :HD], queries, (((1,), (1,)), ((), ())), preferred_element_type=jnp.float32
            )
            if masked:
                pieces = []
                for n in range(count):
                    part = s[n * PIECE : (n + 1) * PIECE]
                    shift = SHIFT[begin + n]
                    if shift == 0:
                        key = lax.broadcasted_iota(jnp.int32, part.shape, 0) + (x_lo * ROWS + half * PIECE)
                        query = lax.rem(lax.broadcasted_iota(jnp.int32, part.shape, 1), ROWS) + core * ROWS
                        pieces.append(jnp.where(key <= query, part, MASKED))
                    else:
                        allowed = lax.rem(z + shift, RING) < z
                        pieces.append(part + jnp.where(allowed, 0.0, MASKED).astype(jnp.float32))
                s = jnp.concatenate(pieces, axis=0)
            scores.append(s)
            values.append(block[:, HD:])
        old = stats[xi, 0:1, :]
        top = old
        for s in scores:
            top = jnp.maximum(top, jnp.max(s, axis=0, keepdims=True))
        factor = jnp.exp2((old - top) * EXP2)
        total = stats[xi, 1:2, :] * factor
        result = acc[xi] * factor
        for s, v in zip(scores, values):
            p = jnp.exp2((s - top) * EXP2)
            total += jnp.sum(p, axis=0, keepdims=True)
            result += lax.dot_general(
                v, p.astype(jnp.bfloat16), (((0,), (0,)), ((), ())), preferred_element_type=jnp.float32
            )
        acc[xi] = result
        stats[xi, 0:1, :] = top
        stats[xi, 1:2, :] = total

    def attend_all(wave):
        @pl.when(x_hi == 0)
        def _():
            @pl.loop(2, 4)
            def _(xi):
                attend(wave, xi, False)

        @pl.loop(0, 2)
        def _(xi):
            attend(wave, xi, True)

    for wave in range(len(WAVES)):
        if wave + 1 < len(WAVES):
            for chunk in WAVES[wave + 1]:
                if chunk[0] == 0:
                    arrived(chunk)
                    if chunk[1] in (5, 3):
                        continue
                    pass_on(chunk[1])
            if wave == 2:
                last = remote(
                    kv.at[core, PLACE[(0, 3)] + other],
                    kv.at[core, PLACE[(0, 4)]],
                    last_send,
                    z_recv.at[PLACE[(0, 4)]],
                    (x_hi * RING + lax.rem(z + 4 - 8 * core + RING, RING), head),
                )
                last.start()
                waiting.append(last)
                pass_on(3)
                pass_on(5)
        for chunk in WAVES[wave]:
            if chunk[0] != 0:
                arrived(chunk)
        exchange(wave)
        if wave == 0:
            own_q.wait()
            for xi, same, copy in q_copies:
                ks = core if same else other
                remote(
                    q.at[xi, ks], q.at[xi, ks], q_send.at[xi, int(same)], q_recv.at[xi, int(same)], along_x(xi, ks)
                ).wait_recv()
        attend_all(wave)

    def give(xi):
        sent[xi] = acc[xi].astype(jnp.bfloat16)
        return [
            remote(sent.at[xi], got.at[xi], merge_send.at[xi, 0], merge_recv.at[xi, 0], along_x(xi, core)),
            remote(stats.at[xi], got_stats.at[xi], merge_send.at[xi, 1], merge_recv.at[xi, 1], along_x(xi, core)),
        ]

    def take(xi):
        return [
            remote(got.at[xi], got.at[xi], merge_send.at[xi, 0], merge_recv.at[xi, 0], along_x(xi, core)),
            remote(got_stats.at[xi], got_stats.at[xi], merge_send.at[xi, 1], merge_recv.at[xi, 1], along_x(xi, core)),
        ]

    for xi in (2, 3, 1):
        for copy in give(xi):
            copy.start()
            waiting.append(copy)
    for xi in (1, 3, 2):
        for copy in take(xi):
            copy.wait_recv()

    tops = [stats[0, 0:1, :]] + [got_stats[xi, 0:1, :] for xi in (1, 2, 3)]
    top = jnp.maximum(jnp.maximum(tops[0], tops[1]), jnp.maximum(tops[2], tops[3]))
    factors = [jnp.exp2((t - top) * EXP2) for t in tops]
    total = stats[0, 1:2, :] * factors[0]
    result = acc[0] * factors[0]
    for xi in (1, 2, 3):
        total += got_stats[xi, 1:2, :] * factors[xi]
        result += got[xi].astype(jnp.float32) * factors[xi]
    turned = jnp.transpose(result / total).astype(jnp.bfloat16)
    attended = jnp.concatenate([turned[n * ROWS : (n + 1) * ROWS] for n in range(4)], axis=1)

    own_w.wait()
    remote(w_in, w.at[other], w_send, w_recv, in_slice(0, other)).wait_recv()
    for i2 in (6, 7, 4, 5, 2, 3, 1, 0):
        chip = in_slice(i2, 0)[1]
        columns = pl.ds(pl.multiple_of(chip * HD, 2 * HD), 2 * HD)
        sums = jnp.dot(attended[:, : 2 * HD], w[0, :, columns], preferred_element_type=jnp.float32)
        sums += jnp.dot(attended[:, 2 * HD :], w[1, :, columns], preferred_element_type=jnp.float32)
        for kd in range(2):
            parts[i2, kd] = sums[:, kd * HD : (kd + 1) * HD].astype(jnp.bfloat16)
        if i2:
            for kd in range(2):
                copy = remote(
                    parts.at[i2, kd],
                    landed.at[i2, core],
                    sum_send.at[i2, kd],
                    sum_recv.at[i2, core],
                    in_slice(i2, kd),
                )
                copy.start()
                waiting.append(copy)
        else:
            copy = remote(
                parts.at[0, other],
                landed.at[0, core],
                sum_send.at[0, 0],
                sum_recv.at[0, core],
                in_slice(0, other),
            )
            copy.start()
            waiting.append(copy)
    landed[0, core] = parts[0, core]
    for i2 in range(8):
        for ks in range(2) if i2 else (other,):
            remote(
                landed.at[i2, ks], landed.at[i2, ks], sum_send.at[i2, 0], sum_recv.at[i2, ks], in_slice(i2, other)
            ).wait_recv()
    for ks in range(2):
        sums = landed[0, ks].astype(jnp.float32)
        for i2 in range(1, 8):
            sums += landed[i2, ks].astype(jnp.float32)
        out[ks * ROWS : (ks + 1) * ROWS] = sums.astype(jnp.bfloat16)
    for copy in waiting:
        copy.wait_send()


def on_device(query_rows, key_rows, value_rows, w_out):
    bf16, f32 = jnp.bfloat16, jnp.float32
    dma = pltpu.SemaphoreType.DMA
    chunks = len(ORDER)
    return pl.pallas_call(
        kernel,
        out_shape=jax.ShapeDtypeStruct((TOK, HD), bf16),
        in_specs=[pl.BlockSpec(memory_space=pl.ANY)] * 4,
        out_specs=pl.BlockSpec(memory_space=pltpu.VMEM),
        scratch_shapes=[
            pltpu.VMEM((2, chunks, PIECE, 2 * HD), bf16),
            pltpu.VMEM((4, 2, ROWS, 2 * HD), bf16),
            pltpu.VMEM((2,) + w_out.shape, bf16),
            pltpu.VMEM((4, HD, COLS), f32),
            pltpu.VMEM((4, 8, COLS), f32),
            pltpu.VMEM((4, HD, COLS), bf16),
            pltpu.VMEM((4, HD, COLS), bf16),
            pltpu.VMEM((4, 8, COLS), f32),
            pltpu.VMEM((8, 2, ROWS, HD), bf16),
            pltpu.VMEM((8, 2, ROWS, HD), bf16),
            dma((4,)),
            dma((chunks,)),
            dma((chunks,)),
            dma,
            dma((len(WAVES),)),
            dma((len(WAVES),)),
            dma((4, 2)),
            dma((4, 2)),
            dma,
            dma,
            dma((4, 2)),
            dma((4, 2)),
            dma((8, 2)),
            dma((8, 2)),
        ],
        compiler_params=pltpu.CompilerParams(
            collective_id=0, has_side_effects=True, vmem_limit_bytes=56 * 1024 * 1024
        ),
        name="attention",
    )(query_rows, key_rows, value_rows, w_out)


def solution(mesh):
    placed = (P("ctx", "head"), P("ctx", None), P("ctx", None), P("head", None))
    return jax.shard_map(
        on_device, mesh=mesh, in_specs=placed, out_specs=P("ctx", "head"), check_vma=False
    )
```

time: 965 us -> 69.2 us (0.07); the launches traced: 951 us -> 69 us
  waiting for transfers between devices: 640 us -> 0 us
  matrix products: 267 us -> 0 us
  Pallas kernels: 0 us -> 67.6 us
  other arithmetic: 17.1 us -> 0 us
  between operations: 13.2 us -> 0.01 us
    all_gather x2 -> x0, waiting for transfers between devices: 554 us -> none  [the longest x1 279 us: on_device(): piece_values = lax.all_gather(own_values, 'ctx', axis=0, tiled=True)]
    dot_general x257 -> x0, matrix products: 267 us -> none  [the longest x128 134 us: attend(): jnp.einsum('thk,kd->thd', weights.astype(jnp.bfloat16), block_values, pre...]
    unnamed x4 -> x0, waiting for transfers between devices: 86.4 us -> none
    pallas_call x0 -> x1, Pallas kernels: none -> 67.6 us  [on_device(): pl.pallas_call(kernel, out_shape=jax.ShapeDtypeStruct((TOK, HD), bf16), i...]
  transfers between devices with their start and end apart: 3 -> 0, of which waited for: 3 -> 0; matrix products, arithmetic and copies ran while one was open for 0% -> 0% of each run, Pallas kernels for 0% -> 0%
where the time goes in v1:
time: 69.2 us; the launch traced here: 69 us
  Pallas kernels  67.6 us (98%)
  local copies, waits for them, and re-layouts  1.42 us (2%)
    pallas_call x1, Pallas kernels, on_device(): pl.pallas_call(kernel, out_shape=jax.ShapeDtypeStruct((TOK, HD), bf16), i...  67.6 us
    unnamed x1, local copies, waits for them, and re-layouts  1.42 us

profile of v1, /device:TPU:1, one launch (start us, length us, event | category | flops | bytes accessed | tf_op | source)
XLA Modules:
  0.0 69.0 jit_solution(14806839037843322906)
XLA Ops:
  0.0 67.6 %attention.1 = bf16[192,128]{1,0:T(8,128)(2,1)} custom-call(bf16[192,256]{1,0:T(8,128)(2,1)} %q_in.1, bf16[192,512]{1,0:T(8,128)(2,1)} %k_in.1, bf16[192,512]{1,0:T(8,128)(2,1)} %v_in.1, bf16[256,2048]{1,0:T(8,128)(2,1)} %w_in.1), custom_call_target="tpu_custom_call" | custom-call | tf_op jit(solution)/shard_map/attention/pallas_call | solution.py:327
  67.6 1.4 %copy.6 = bf16[192,128]{1,0:T(8,128)(2,1)} copy(bf16[192,128]{1,0:T(8,128)(2,1)} %attention.1) | data formatting | bytes 98304

commit v2 on v1

--- a/solution.py
+++ b/solution.py
@@ -23,8 +23,8 @@
     [(0, 0), (1, 0), (3, 0), (2, 0), (2, 7)],
     [(0, 1), (0, 7), (1, 1), (1, 7), (3, 1), (3, 7), (2, 1), (2, 6)],
     [(0, 2), (0, 6), (1, 2), (1, 6), (3, 2), (3, 6), (2, 2), (2, 5)],
-    [(0, 3), (0, 5), (1, 3), (1, 5), (3, 3), (3, 5), (2, 3), (2, 4)],
-    [(0, 4), (1, 4), (3, 4)],
+    [(0, 3), (0, 5), (1, 3), (1, 5), (3, 3), (3, 5)],
+    [(2, 3), (2, 4), (1, 4), (3, 4), (0, 4)],
 ]
 ORDER = [chunk for wave in WAVES for chunk in wave]
 PLACE = {chunk: place for place, chunk in enumerate(ORDER)}
@@ -33,7 +33,13 @@
 
 
 def near(slot):
+    if slot == 4:
+        return []
     steps = [(1, (3, slot)), (-1, (1, slot))]
+    if slot == 5:
+        steps.append((3, (1, 4)))
+    if slot == 3:
+        steps.append((-3, (3, 4)))
     if slot in (0, 7, 6, 5):
         steps.append((2, (2, (slot - 1) % 8)))
     if slot in (0, 1, 2, 3):
@@ -42,8 +48,8 @@
 
 
 def kernel(
-    q_in, k_in, v_in, w_in, out,
-    kv, q, w, acc, stats, sent, got, got_stats, parts, landed,
+    q_in, k_in, v_in, w_in, landed,
+    kv, q, w, acc, stats, sent, got, got_stats, parts,
     load_sem, z_send, z_recv, last_send, pair_send, pair_recv, q_send, q_recv, w_send, w_recv,
     merge_send, merge_recv, sum_send, sum_recv,
 ):
@@ -87,17 +93,16 @@
         q_in.at[pl.ds(pl.multiple_of(core * ROWS, 16), ROWS)], q.at[0, core], load_sem.at[2]
     )
     own_w = pltpu.make_async_copy(w_in, w.at[core], load_sem.at[3])
+    barrier = pltpu.get_barrier_semaphore()
+    peers = [along_z(step) for step in (4, -4, 3, -3, 2, -2, 1, -1)]
+    peers += [along_x(xi, kd) for xi in (2, 3) for kd in (core, other)]
+    peers += [in_slice(i2, kd) for i2 in range(8) for kd in (core, other) if (i2, kd is core) != (0, True)]
+    for peer in peers:
+        pl.semaphore_signal(barrier, inc=1, device_id=peer, device_id_type=MESH)
     own_k.start()
     own_v.start()
     own_q.start()
     own_w.start()
-
-    barrier = pltpu.get_barrier_semaphore()
-    peers = [along_z(step) for step in (4, -4, 2, -2, 1, -1)]
-    peers += [along_x(xi, kd) for xi in (2, 3) for kd in (core, other)]
-    peers += [in_slice(i2, kd) for i2 in range(8) for kd in (core, other) if (i2, kd is core) != (0, True)]
-    for peer in peers:
-        pl.semaphore_signal(barrier, inc=1, device_id=peer, device_id_type=MESH)
     acc[...] = jnp.zeros_like(acc)
     row = lax.broadcasted_iota(jnp.int32, stats.shape, 1)
     stats[...] = jnp.where(row == 0, FLOOR, 0.0).astype(jnp.float32)
@@ -153,6 +158,9 @@
         copy = remote(piece, piece, pair_send.at[wave], pair_recv.at[wave], in_slice(0, other))
         copy.start()
         waiting.append(copy)
+
+    def exchanged(wave):
+        begin, count = PLACE[WAVES[wave][0]], len(WAVES[wave])
         theirs = kv.at[other, pl.ds(begin, count)]
         remote(theirs, theirs, pair_send.at[wave], pair_recv.at[wave], in_slice(0, other)).wait_recv()
 
@@ -206,14 +214,21 @@
             def _(xi):
                 attend(wave, xi, False)
 
-        @pl.loop(0, 2)
-        def _(xi):
-            attend(wave, xi, True)
+        reached = wave == 0
+        for place in range(PLACE[WAVES[wave][0]], PLACE[WAVES[wave][0]] + len(WAVES[wave])):
+            if SHIFT[place]:
+                reached |= lax.rem(z + SHIFT[place], RING) < z
+
+        @pl.when(reached)
+        def _():
+            @pl.loop(0, 2)
+            def _(xi):
+                attend(wave, xi, True)
 
     for wave in range(len(WAVES)):
         if wave + 1 < len(WAVES):
             for chunk in WAVES[wave + 1]:
-                if chunk[0] == 0:
+                if chunk[0] == 0 and chunk[1] != 4:
                     arrived(chunk)
                     if chunk[1] in (5, 3):
                         continue
@@ -231,7 +246,7 @@
                 pass_on(3)
                 pass_on(5)
         for chunk in WAVES[wave]:
-            if chunk[0] != 0:
+            if chunk[0] or chunk[1] == 4:
                 arrived(chunk)
         exchange(wave)
         if wave == 0:
@@ -241,10 +256,17 @@
                 remote(
                     q.at[xi, ks], q.at[xi, ks], q_send.at[xi, int(same)], q_recv.at[xi, int(same)], along_x(xi, ks)
                 ).wait_recv()
-        attend_all(wave)
-
-    def give(xi):
-        sent[xi] = acc[xi].astype(jnp.bfloat16)
+        else:
+            exchanged(wave - 1)
+            attend_all(wave - 1)
+    exchanged(len(WAVES) - 1)
+    attend_all(len(WAVES) - 1)
+
+    def give(xi, wanted):
+        @pl.when(wanted)
+        def _():
+            sent[xi] = acc[xi].astype(jnp.bfloat16)
+
         return [
             remote(sent.at[xi], got.at[xi], merge_send.at[xi, 0], merge_recv.at[xi, 0], along_x(xi, core)),
             remote(stats.at[xi], got_stats.at[xi], merge_send.at[xi, 1], merge_recv.at[xi, 1], along_x(xi, core)),
@@ -256,23 +278,30 @@
             remote(got_stats.at[xi], got_stats.at[xi], merge_send.at[xi, 1], merge_recv.at[xi, 1], along_x(xi, core)),
         ]
 
-    for xi in (2, 3, 1):
-        for copy in give(xi):
-            copy.start()
-            waiting.append(copy)
-    for xi in (1, 3, 2):
+    from_low = [copy for xi in (2, 3) for copy in give(xi, x_hi == 0)]
+    pl.when(x_hi == 0)(lambda: [copy.start() for copy in from_low] and None)
+    for copy in give(1, True):
+        copy.start()
+        waiting.append(copy)
+
+    def absorb(xi):
         for copy in take(xi):
             copy.wait_recv()
-
-    tops = [stats[0, 0:1, :]] + [got_stats[xi, 0:1, :] for xi in (1, 2, 3)]
-    top = jnp.maximum(jnp.maximum(tops[0], tops[1]), jnp.maximum(tops[2], tops[3]))
-    factors = [jnp.exp2((t - top) * EXP2) for t in tops]
-    total = stats[0, 1:2, :] * factors[0]
-    result = acc[0] * factors[0]
-    for xi in (1, 2, 3):
-        total += got_stats[xi, 1:2, :] * factors[xi]
-        result += got[xi].astype(jnp.float32) * factors[xi]
-    turned = jnp.transpose(result / total).astype(jnp.bfloat16)
+        mine, theirs = stats[0, 0:1, :], got_stats[xi, 0:1, :]
+        top = jnp.maximum(mine, theirs)
+        mine, theirs = jnp.exp2((mine - top) * EXP2), jnp.exp2((theirs - top) * EXP2)
+        acc[0] = acc[0] * mine + got[xi].astype(jnp.float32) * theirs
+        stats[0, 1:2, :] = stats[0, 1:2, :] * mine + got_stats[xi, 1:2, :] * theirs
+        stats[0, 0:1, :] = top
+
+    absorb(1)
+
+    @pl.when(x_hi == 1)
+    def _():
+        absorb(3)
+        absorb(2)
+
+    turned = jnp.transpose(acc[0] / stats[0, 1:2, :]).astype(jnp.bfloat16)
     attended = jnp.concatenate([turned[n * ROWS : (n + 1) * ROWS] for n in range(4)], axis=1)
 
     own_w.wait()
@@ -305,30 +334,28 @@
             )
             copy.start()
             waiting.append(copy)
-    landed[0, core] = parts[0, core]
+    keep = pltpu.make_async_copy(parts.at[0, core], landed.at[0, core], load_sem.at[4])
+    keep.start()
     for i2 in range(8):
         for ks in range(2) if i2 else (other,):
             remote(
                 landed.at[i2, ks], landed.at[i2, ks], sum_send.at[i2, 0], sum_recv.at[i2, ks], in_slice(i2, other)
             ).wait_recv()
-    for ks in range(2):
-        sums = landed[0, ks].astype(jnp.float32)
-        for i2 in range(1, 8):
-            sums += landed[i2, ks].astype(jnp.float32)
-        out[ks * ROWS : (ks + 1) * ROWS] = sums.astype(jnp.bfloat16)
+    keep.wait()
     for copy in waiting:
         copy.wait_send()
+    pl.when(x_hi == 0)(lambda: [copy.wait_send() for copy in from_low] and None)
 
 
 def on_device(query_rows, key_rows, value_rows, w_out):
     bf16, f32 = jnp.bfloat16, jnp.float32
     dma = pltpu.SemaphoreType.DMA
     chunks = len(ORDER)
-    return pl.pallas_call(
+    landed = pl.pallas_call(
         kernel,
-        out_shape=jax.ShapeDtypeStruct((TOK, HD), bf16),
+        out_shape=jax.ShapeDtypeStruct((8, 2, ROWS, HD), bf16),
         in_specs=[pl.BlockSpec(memory_space=pl.ANY)] * 4,
-        out_specs=pl.BlockSpec(memory_space=pltpu.VMEM),
+        out_specs=pl.BlockSpec(memory_space=pl.ANY),
         scratch_shapes=[
             pltpu.VMEM((2, chunks, PIECE, 2 * HD), bf16),
             pltpu.VMEM((4, 2, ROWS, 2 * HD), bf16),
@@ -339,8 +366,7 @@
             pltpu.VMEM((4, HD, COLS), bf16),
             pltpu.VMEM((4, 8, COLS), f32),
             pltpu.VMEM((8, 2, ROWS, HD), bf16),
-            pltpu.VMEM((8, 2, ROWS, HD), bf16),
-            dma((4,)),
+            dma((5,)),
             dma((chunks,)),
             dma((chunks,)),
             dma,
@@ -360,6 +386,7 @@
         ),
         name="attention",
     )(query_rows, key_rows, value_rows, w_out)
+    return jnp.sum(landed.astype(f32), axis=0).astype(bf16).reshape(TOK, HD)
 
 
 def solution(mesh):

time: 69.2 us -> 65.4 us (0.945)
  Pallas kernels: 67.6 us -> 63.5 us
  other arithmetic: 0 us -> 1.69 us
  local copies, waits for them, and re-layouts: 1.42 us -> 0 us
    pallas_call x1, Pallas kernels: 67.6 us -> 63.5 us  [on_device(): pl.pallas_call(kernel, out_shape=jax.ShapeDtypeStruct((8, 2, ROWS, HD), b...]
    reduce_sum x0 -> x1, other arithmetic: none -> 1.69 us  [on_device(): return jnp.sum(landed.astype(f32), axis=0).astype(bf16).reshape(TOK, HD)]
    unnamed x1 -> x0, local copies, waits for them, and re-layouts: 1.42 us -> none
where the time goes in v2:
time: 65.4 us; the launch traced here: 65.2 us
  Pallas kernels  63.5 us (97%)
  other arithmetic  1.69 us (3%)
    pallas_call x1, Pallas kernels, on_device(): pl.pallas_call(kernel, out_shape=jax.ShapeDtypeStruct((8, 2, ROWS, HD), b...  63.5 us
    reduce_sum x1, other arithmetic, on_device(): return jnp.sum(landed.astype(f32), axis=0).astype(bf16).reshape(TOK, HD)  1.69 us

profile of v2, /device:TPU:1, one launch (start us, length us, event | category | flops | bytes accessed | tf_op | source)
XLA Modules:
  0.0 65.2 jit_solution(9177526013883585015)
XLA Ops:
  0.0 63.5 %attention.1 = bf16[8,2,96,128]{3,2,1,0:T(8,128)(2,1)} custom-call(bf16[192,256]{1,0:T(8,128)(2,1)} %q_in.1, bf16[192,512]{1,0:T(8,128)(2,1)} %k_in.1, bf16[192,512]{1,0:T(8,128)(2,1)} %v_in.1, bf16[256,2048]{1,0:T(8,128)(2,1)} %w_in.1), custom_call_target="tpu_custom_call" | custom-call | tf_op jit(solution)/shard_map/attention/pallas_call | solution.py:354
  63.5 1.7 %reduce_sum.12 = bf16[2,96,128]{2,1,0:T(8,128)(2,1)} reduce(bf16[8,2,96,128]{3,2,1,0:T(8,128)(2,1)} %attention.1, bf16[]{:T(256)} %constant.2.clone.1), dimensions={0}, to_apply=%region_0.0 | reduce | flops 172032 | bytes 442370 | tf_op jit(solution)/shard_map/reduce_sum | solution.py:389

commit v3 on v2

--- a/solution.py
+++ b/solution.py
@@ -225,6 +225,23 @@
             def _(xi):
                 attend(wave, xi, True)
 
+    def collect(wave):
+        for chunk in WAVES[wave]:
+            if chunk[0] or chunk[1] == 4:
+                arrived(chunk)
+        exchange(wave)
+
+    def use(wave):
+        exchanged(wave)
+        if wave == 0:
+            own_q.wait()
+            for xi, same, copy in q_copies:
+                ks = core if same else other
+                remote(
+                    q.at[xi, ks], q.at[xi, ks], q_send.at[xi, int(same)], q_recv.at[xi, int(same)], along_x(xi, ks)
+                ).wait_recv()
+        attend_all(wave)
+
     for wave in range(len(WAVES)):
         if wave + 1 < len(WAVES):
             for chunk in WAVES[wave + 1]:
@@ -245,22 +262,13 @@
                 waiting.append(last)
                 pass_on(3)
                 pass_on(5)
-        for chunk in WAVES[wave]:
-            if chunk[0] or chunk[1] == 4:
-                arrived(chunk)
-        exchange(wave)
-        if wave == 0:
-            own_q.wait()
-            for xi, same, copy in q_copies:
-                ks = core if same else other
-                remote(
-                    q.at[xi, ks], q.at[xi, ks], q_send.at[xi, int(same)], q_recv.at[xi, int(same)], along_x(xi, ks)
-                ).wait_recv()
-        else:
-            exchanged(wave - 1)
-            attend_all(wave - 1)
-    exchanged(len(WAVES) - 1)
-    attend_all(len(WAVES) - 1)
+        if wave >= 1:
+            collect(wave - 1)
+        if wave >= 2:
+            use(wave - 2)
+    collect(len(WAVES) - 1)
+    use(len(WAVES) - 2)
+    use(len(WAVES) - 1)
 
     def give(xi, wanted):
         @pl.when(wanted)

time: 65.4 us -> 65.2 us (level)
  no operation moved by 1% of the time
where the time goes in v3:
time: 65.2 us; the launch traced here: 65 us
  Pallas kernels  63.4 us (97%)
  other arithmetic  1.69 us (3%)
    pallas_call x1, Pallas kernels, on_device(): pl.pallas_call(kernel, out_shape=jax.ShapeDtypeStruct((8, 2, ROWS, HD), b...  63.4 us
    reduce_sum x1, other arithmetic, on_device(): return jnp.sum(landed.astype(f32), axis=0).astype(bf16).reshape(TOK, HD)  1.69 us

profile of v3, /device:TPU:1, one launch (start us, length us, event | category | flops | bytes accessed | tf_op | source)
XLA Modules:
  0.0 65.0 jit_solution(10792278379673995114)
XLA Ops:
  0.0 63.4 %attention.1 = bf16[8,2,96,128]{3,2,1,0:T(8,128)(2,1)} custom-call(bf16[192,256]{1,0:T(8,128)(2,1)} %q_in.1, bf16[192,512]{1,0:T(8,128)(2,1)} %k_in.1, bf16[192,512]{1,0:T(8,128)(2,1)} %v_in.1, bf16[256,2048]{1,0:T(8,128)(2,1)} %w_in.1), custom_call_target="tpu_custom_call" | custom-call | tf_op jit(solution)/shard_map/attention/pallas_call | solution.py:362
  63.4 1.7 %reduce_sum.12 = bf16[2,96,128]{2,1,0:T(8,128)(2,1)} reduce(bf16[8,2,96,128]{3,2,1,0:T(8,128)(2,1)} %attention.1, bf16[]{:T(256)} %constant.2.clone.1), dimensions={0}, to_apply=%region_0.0 | reduce | flops 172032 | bytes 442370 | tf_op jit(solution)/shard_map/reduce_sum | solution.py:397
